TPU v7x, 32 devices: a whole 2x2x4 slice. The times are simulated.
32 devices in a mesh: groups: 2 (over y), freq: 4 (over z), rows: 4 (over x, core).
Axes of the slice: x: 2, y: 2, z: 4, core: 2. Of those that a mesh axis runs over, the one named last changes fastest.
Arguments:
- traces: bfloat16 [8192, 32, 1024], P(('groups', 'freq'), 'rows'), parts along dimension 0, may hold values from -6 to 6
- tile_ranks: int32 [8, 16, 16], P(('groups', 'freq'), 'rows'), parts along dimension 0, may hold values from 8 to 32, as said below
- source_map: int32 [8192], P('groups'), parts along dimension 0, may hold values from 0 to 4095, as said below
- receiver_map: int32 [8192], P(('groups', 'rows')), parts along dimension 0, may hold values from 0 to 4095, as said below
- left_factors: float32 [2, 8, 16, 256, 512], P(None, ('groups', 'freq'), 'rows'), parts along dimension 1, may hold values from -0.3125 to 0.3125
- right_factors: float32 [2, 8, 16, 512, 256], P(None, ('groups', 'freq'), 'rows'), parts along dimension 1, may hold values from -0.375 to 0.375
Outputs:
- convolved: bfloat16 [8, 1024, 32, 1024], P(('groups', 'rows'), 'freq'), parts along dimension 0
There are 2 independent parts, one for each index of `groups`. A program takes and returns all parts, laid end to end along the dimension named above; each array names one. Nothing has to cross between parts.
Inputs may be any that keep to these rules, and one draw needn't show every extreme that they name: `tile_ranks`: multiples of 8. For every frequency, the ranks of each tile row sum to at most 512, and some tile row has all its ranks equal to 32. `source_map`: A permutation of the slab's sources. `receiver_map`: each aligned block of 1024 entries is a permutation of that block's own indices.
All inputs are finite; a program needn't handle non-finite values.
Results may differ from a plain program's by a relative error of at most 0.0043.
Values sent between devices are 32-bit elements; how exact they have to be, the bound alone decides.
A program may use at most 192 MiB of HBM per device.

v0:
```python
import functools
import math

import jax
import jax.numpy as jnp
import numpy as np
from jax import lax
from jax.experimental import pallas as pl
from jax.experimental.pallas import tpu as pltpu
from jax.sharding import PartitionSpec as P

RMAX = 32
MESH = pl.DeviceIdType.MESH
VMEM_LIMIT = 52 * 1024 * 1024


def tables(samples, bins):
    turns = (np.arange(bins)[:, None] + 1) * np.arange(samples)[None, :] % samples
    angles = turns.astype(np.float32) * np.float32(2.0 * math.pi / samples)
    return np.stack([np.cos(angles), -np.sin(angles)], axis=1).astype(np.float32)


def round_up(value, unit):
    return -(-value // unit) * unit


def row_messages(n_rows):
    known, messages = [0], []
    for bit in reversed(range(n_rows.bit_length() - 1)):
        messages += [(1 << bit, off) for off in known]
        known += [off ^ (1 << bit) for off in known]
    return messages


def spectra_kernel(nf, n_rows, chunks, x_ref, w_ref, t_ref, xbuf, sv, spec, land,
                   in_sem, s1_send, s1_recv, h_send, h_recv):
    z, r = lax.axis_index("freq"), lax.axis_index("rows")
    width, members = xbuf.shape[1], xbuf.shape[2]
    samples = xbuf.shape[3]
    lanes = w_ref.shape[1]
    sources = width * chunks
    messages = row_messages(n_rows)
    pair = 2 * members

    loads = []
    for c in range(chunks):
        load = pltpu.make_async_copy(x_ref.at[pl.ds(c * width, width)], xbuf.at[c], in_sem.at[c])
        load.start()
        loads.append(load)

    barrier = pltpu.get_barrier_semaphore()
    bits = [1 << b for b in range(n_rows.bit_length() - 1)]
    for d in range(1, nf):
        pl.semaphore_signal(barrier, inc=1, device_id={"freq": lax.rem(z + d, nf)}, device_id_type=MESH)
    for bit in bits:
        flip = r + bit - 2 * bit * lax.rem(r // bit, 2)
        pl.semaphore_signal(barrier, inc=1, device_id={"rows": flip}, device_id_type=MESH)
    pl.semaphore_wait(barrier, nf - 1 + len(bits))

    def flipped(index, mask):
        for bit in bits:
            if mask & bit:
                index = index + bit - 2 * bit * lax.rem(index // bit, 2)
        return index

    def band_copy(c, d):
        to = lax.rem(z + d, nf)
        return pltpu.make_async_remote_copy(
            src_ref=spec.at[c, to], dst_ref=land.at[c, r, z],
            send_sem=s1_send.at[c, d], recv_sem=s1_recv.at[c, d],
            device_id={"freq": to}, device_id_type=MESH)

    def row_copy(c, m):
        bit, off = messages[m]
        block = land.at[c, flipped(r, off)]
        return pltpu.make_async_remote_copy(
            src_ref=block, dst_ref=block,
            send_sem=h_send.at[c, m], recv_sem=h_recv.at[c, m],
            device_id={"rows": flipped(r, bit)}, device_id_type=MESH)

    def compute(c):
        piece = 128
        lane_v = lax.rem(lax.broadcasted_iota(jnp.int32, (piece, 128), 1), members)
        for s0 in range(0, width, piece):
            block = xbuf[c, s0:s0 + piece].reshape(piece * members, samples)
            found = jnp.dot(block, w_ref[...], preferred_element_type=jnp.float32)
            for tile in range(lanes // 128):
                sv[tile] = found[:, tile * 128:(tile + 1) * 128]
                picked = sv[tile, pl.ds(0, piece, stride=members), :]
                for v in range(1, members):
                    picked = jnp.where(lane_v == v, sv[tile, pl.ds(v, piece, stride=members), :], picked)
                turned = picked.T
                per_tile = 128 // pair
                for f in range(tile * per_tile, min(nf, (tile + 1) * per_tile)):
                    here = (f - tile * per_tile) * pair
                    spec[c, f, :, s0:s0 + piece] = turned[here:here + pair]
        land[c, r, z] = spec[c, z]
        for d in range(1, nf):
            band_copy(c, d).start()

    def turn(c):
        for zz in range(nf):
            parts = [land[c, rr, zz] for rr in range(n_rows)]
            again = []
            for part in parts:
                again += [-part[members:], part[:members]]
            full = jnp.concatenate(parts + again, axis=0)
            t_ref[zz * sources + c * width:zz * sources + (c + 1) * width, :] = full.T

    stages = []
    for m, (bit, off) in enumerate(messages):
        stage = 0 if off == 0 else bits.__len__() - (off & -off).bit_length() + 1
        stages.append(stage)
    depth = len(bits)
    for step in range(chunks + depth + 1):
        if step < chunks:
            loads[step].wait()
            compute(step)
        for stage in range(depth + 1):
            c = step - 1 - stage
            if not 0 <= c < chunks:
                continue
            if stage == 0:
                for d in range(1, nf):
                    band_copy(c, d).wait_recv()
            else:
                done_bit = bits[depth - stage]
                for m, (bit, off) in enumerate(messages):
                    if bit == done_bit:
                        row_copy(c, m).wait_recv()
            for m in range(len(messages)):
                if stages[m] == stage:
                    row_copy(c, m).start()
            if stage == depth:
                turn(c)
    for c in range(chunks):
        for d in range(1, nf):
            band_copy(c, d).wait_send()
        for m in range(len(messages)):
            row_copy(c, m).wait_send()


def image_kernel(t_ref, smap, rmap, ranks, left, right, o_ref, cols, lbuf, rbuf, proj, img, even, odd, l_sem, r_sem):
    slab = cols.shape[0]
    tile_rows, blocks = ranks.shape[1], ranks.shape[2]
    capacity, tile = right.shape[3], right.shape[4]
    receivers = img.shape[0]
    loads_r = [[pltpu.make_async_copy(right.at[c, 0, i], rbuf.at[c, i, pl.ds(0, capacity)], r_sem.at[c, i])
                for i in range(tile_rows)] for c in range(2)]
    loads_l = [[pltpu.make_async_copy(left.at[c, 0, i], lbuf.at[c, i], l_sem.at[c, i])
                for i in range(tile_rows)] for c in range(2)]
    for loads in (loads_r, loads_l):
        for i in range(tile_rows):
            for c in range(2):
                loads[c][i].start()
    proj[...] = jnp.zeros_like(proj)

    @pl.loop(0, slab // 16)
    def _(g):
        for u in range(16):
            q = g * 16 + u
            cols[pl.ds(q, 1), :] = t_ref[pl.ds(smap[q], 1), :]

    for i in range(tile_rows):
        for c in range(2):
            loads_r[c][i].wait()
    lane = lax.broadcasted_iota(jnp.int32, (tile_rows * RMAX, 128), 1)
    sign = jnp.where(lane < 64, -1.0, 1.0)
    starts = [jnp.int32(0)] * tile_rows
    for j in range(blocks):
        col = cols[j * tile:(j + 1) * tile, :].astype(jnp.bfloat16)
        at = [pl.multiple_of(s, 8) for s in starts]
        both = [jnp.concatenate([rbuf[c, i, pl.ds(at[i], RMAX), :] for i in range(tile_rows)], axis=0)
                .astype(jnp.bfloat16) for c in range(2)]
        first = jnp.dot(both[0], col, preferred_element_type=jnp.float32)
        second = jnp.dot(both[1], col, preferred_element_type=jnp.float32)
        total = first + sign * pltpu.roll(second, 64, 1)
        for i in range(tile_rows):
            proj[i, pl.ds(at[i], RMAX), :] = total[i * RMAX:(i + 1) * RMAX]
            starts[i] = starts[i] + ranks[0, i, j]
    for i in range(tile_rows):
        proj[i, pl.ds(pl.multiple_of(starts[i], 8), RMAX), :] = jnp.zeros((RMAX, 128), jnp.float32)
    for i in range(tile_rows):
        p = proj[i, :capacity, :]
        high = p.astype(jnp.bfloat16)
        low = (p - high.astype(jnp.float32)).astype(jnp.bfloat16)
        wide = jnp.concatenate([high, low], axis=1)
        sums = []
        for c in range(2):
            loads_l[c][i].wait()
            prod = jnp.dot(lbuf[c, i].astype(jnp.bfloat16), wide, preferred_element_type=jnp.float32)
            sums.append(prod[:, :128] + prod[:, 128:])
        img[i * tile:(i + 1) * tile, :] = sums[0] + pltpu.roll(sums[1], 64, 1)

    @pl.loop(0, receivers // 16)
    def _(g):
        for u in range(8):
            n = g * 16 + 2 * u
            even[pl.ds(g * 8 + u, 1), :] = img[pl.ds(lax.rem(rmap[n], receivers), 1), :]
            odd[pl.ds(g * 8 + u, 1), :] = img[pl.ds(lax.rem(rmap[n + 1], receivers), 1), :]

    lane2 = lax.broadcasted_iota(jnp.int32, even.shape, 1)
    o_ref[...] = jnp.where(lane2 < 64, even[...], pltpu.roll(odd[...], 64, 1)).reshape(o_ref.shape)


def return_kernel(nf, i_ref, o_ref, own_sem, send_sem, recv_sem):
    z = lax.axis_index("freq")
    own = pltpu.make_async_copy(i_ref.at[z], o_ref.at[z], own_sem)
    own.start()
    barrier = pltpu.get_barrier_semaphore()
    for d in range(1, nf):
        pl.semaphore_signal(barrier, inc=1, device_id={"freq": lax.rem(z + d, nf)}, device_id_type=MESH)
    pl.semaphore_wait(barrier, nf - 1)
    copies = []
    for d in range(1, nf):
        to = lax.rem(z + d, nf)
        copy = pltpu.make_async_remote_copy(
            src_ref=i_ref.at[to], dst_ref=o_ref.at[z],
            send_sem=send_sem.at[d], recv_sem=recv_sem.at[d],
            device_id={"freq": to}, device_id_type=MESH)
        copy.start()
        copies.append(copy)
    own.wait()
    for copy in copies:
        copy.wait()


def waves_kernel(nf, members, x_ref, w_ref, o_ref, rows, lhs):
    pairs = x_ref.shape[1]
    wide = w_ref.shape[0]
    groups = members // 8
    lane = lax.broadcasted_iota(jnp.int32, (pairs, 128), 1)
    units = [(part, f) for part in (0, 0, 1) for f in range(nf)]
    pieces = []
    for f in range(nf):
        x = x_ref[f]
        high = x.astype(jnp.bfloat16).astype(jnp.float32)
        pieces.append((high, x - high))
    for parity in range(2):
        for g in range(groups):
            base = 64 * parity + 16 * g
            for tile in range(wide // 128):
                acc = jnp.zeros((pairs, 128), jnp.float32)
                for slot, (part, f) in enumerate(units[tile * 8:tile * 8 + 8]):
                    shift = (16 * slot - base) % 128
                    value = pieces[f][part]
                    if shift:
                        value = pltpu.roll(value, shift, 1)
                    acc = jnp.where(lane // 16 == slot, value, acc)
                rows[parity, g, :, tile * 128:tile * 128 + 128] = acc
    sub = lax.broadcasted_iota(jnp.int32, (8, wide), 0)
    keep = lax.rem(lax.broadcasted_iota(jnp.int32, (8, wide), 1), 8) == sub
    for n in range(2 * pairs):
        parts = []
        for g in range(groups):
            row = rows[n % 2, g, pl.ds(n // 2, 1), :]
            parts.append(jnp.where(keep, jnp.broadcast_to(row, (8, wide)), 0.0))
        lhs[n * members:(n + 1) * members, :] = jnp.concatenate(parts, axis=0).astype(jnp.bfloat16)
    step = 4
    for n in range(0, 2 * pairs, step):
        out = jnp.dot(lhs[n * members:(n + step) * members, :], w_ref[...], preferred_element_type=jnp.float32)
        o_ref[0, n:n + step] = out.astype(jnp.bfloat16).reshape(step, members, out.shape[1])


def per_device(traces, tile_ranks, source_map, receiver_map, left_factors, right_factors):
    sources, members, samples = traces.shape
    nf, n_rows = lax.axis_size("freq"), lax.axis_size("rows")
    slab = source_map.shape[0]
    receivers = receiver_map.shape[0]
    all_members = members * n_rows
    tile_rows, capacity, tile = right_factors.shape[2:]
    chunks = max(1, sources // 256)
    width = sources // chunks
    basis = tables(samples, nf)

    forward = (basis / np.float32(math.sqrt(samples))).astype(jnp.bfloat16)
    lanes = round_up(2 * nf * members, 128)
    w = np.zeros((samples, lanes), jnp.bfloat16)
    w[:, :2 * nf * members] = np.repeat(forward.reshape(2 * nf, samples), members, axis=0).T
    n_msg = n_rows - 1
    turned = pl.pallas_call(
        functools.partial(spectra_kernel, nf, n_rows, chunks),
        out_shape=jax.ShapeDtypeStruct((slab, 128), jnp.float32),
        in_specs=[pl.BlockSpec(memory_space=pl.ANY), pl.BlockSpec(memory_space=pltpu.VMEM)],
        out_specs=pl.BlockSpec(memory_space=pltpu.VMEM),
        scratch_shapes=[
            pltpu.VMEM((chunks, width, members, samples), jnp.bfloat16),
            pltpu.VMEM((lanes // 128, 128 * members, 128), jnp.float32),
            pltpu.VMEM((chunks, nf, 2 * members, width), jnp.float32),
            pltpu.VMEM((chunks, n_rows, nf, 2 * members, width), jnp.float32),
            pltpu.SemaphoreType.DMA((chunks,)),
            pltpu.SemaphoreType.DMA((chunks, nf)),
            pltpu.SemaphoreType.DMA((chunks, nf)),
            pltpu.SemaphoreType.DMA((chunks, n_msg)),
            pltpu.SemaphoreType.DMA((chunks, n_msg)),
        ],
        compiler_params=pltpu.CompilerParams(
            collective_id=0, has_side_effects=True, vmem_limit_bytes=VMEM_LIMIT),
        name="spectra",
    )(traces, jnp.asarray(w))

    per = receivers // nf
    image = pl.pallas_call(
        image_kernel,
        out_shape=jax.ShapeDtypeStruct((nf, per // 2, 128), jnp.float32),
        in_specs=[
            pl.BlockSpec(memory_space=pltpu.VMEM),
            pl.BlockSpec(memory_space=pltpu.SMEM),
            pl.BlockSpec(memory_space=pltpu.SMEM),
            pl.BlockSpec(memory_space=pltpu.SMEM),
            pl.BlockSpec(memory_space=pl.ANY),
            pl.BlockSpec(memory_space=pl.ANY),
        ],
        out_specs=pl.BlockSpec(memory_space=pltpu.VMEM),
        scratch_shapes=[
            pltpu.VMEM((slab, 128), jnp.float32),
            pltpu.VMEM((2, tile_rows, tile, capacity), jnp.float32),
            pltpu.VMEM((2, tile_rows, capacity + RMAX, tile), jnp.float32),
            pltpu.VMEM((tile_rows, capacity + RMAX, 128), jnp.float32),
            pltpu.VMEM((receivers, 128), jnp.float32),
            pltpu.VMEM((receivers // 2, 128), jnp.float32),
            pltpu.VMEM((receivers // 2, 128), jnp.float32),
            pltpu.SemaphoreType.DMA((2, tile_rows)),
            pltpu.SemaphoreType.DMA((2, tile_rows)),
        ],
        compiler_params=pltpu.CompilerParams(vmem_limit_bytes=VMEM_LIMIT),
        name="image",
    )(turned, source_map, receiver_map, tile_ranks, left_factors, right_factors)

    returned = pl.pallas_call(
        functools.partial(return_kernel, nf),
        out_shape=jax.ShapeDtypeStruct(image.shape, jnp.float32),
        in_specs=[pl.BlockSpec(memory_space=pltpu.VMEM)],
        out_specs=pl.BlockSpec(memory_space=pltpu.VMEM),
        scratch_shapes=[
            pltpu.SemaphoreType.DMA(()),
            pltpu.SemaphoreType.DMA((nf,)),
            pltpu.SemaphoreType.DMA((nf,)),
        ],
        compiler_params=pltpu.CompilerParams(collective_id=1, has_side_effects=True),
        name="giveback",
    )(image)

    inverse = (basis / np.float32(math.sqrt(nf))).astype(np.float32)
    high = inverse.astype(jnp.bfloat16)
    low = (inverse - high.astype(np.float32)).astype(jnp.bfloat16)
    wide = round_up(3 * nf * 16, 128)
    wb = np.zeros((wide, samples), jnp.bfloat16)
    for part, table in enumerate((high, low, high)):
        wb[part * nf * 16:(part + 1) * nf * 16] = np.repeat(table.reshape(2 * nf, samples), 8, axis=0)
    nb = 16
    return pl.pallas_call(
        functools.partial(waves_kernel, nf, all_members),
        grid=(per // nb,),
        out_shape=jax.ShapeDtypeStruct((1, per, all_members, samples), jnp.bfloat16),
        in_specs=[
            pl.BlockSpec((nf, nb // 2, 128), lambda i: (0, i, 0)),
            pl.BlockSpec((wide, samples), lambda i: (0, 0)),
        ],
        out_specs=pl.BlockSpec((1, nb, all_members, samples), lambda i: (0, i, 0, 0)),
        scratch_shapes=[
            pltpu.VMEM((2, all_members // 8, nb // 2, wide), jnp.float32),
            pltpu.VMEM((nb * all_members, wide), jnp.bfloat16),
        ],
        compiler_params=pltpu.CompilerParams(vmem_limit_bytes=VMEM_LIMIT),
        name="waves",
    )(returned, jnp.asarray(wb))


def solution(mesh):
    return jax.shard_map(
        per_device,
        mesh=mesh,
        in_specs=(
            P(("groups", "freq"), "rows", None),
            P(("groups", "freq"), "rows", None),
            P("groups"),
            P(("groups", "rows")),
            P(None, ("groups", "freq"), "rows", None, None),
            P(None, ("groups", "freq"), "rows", None, None),
        ),
        out_specs=P(("groups", "rows"), "freq", None, None),
        check_vma=False,
    )
```

profile of v0, /device:TPU:0, one launch (start us, length us, event | category | flops | bytes accessed | tf_op | source)
XLA Modules:
  0.0 63.2 jit_solution(18286932526464048511)
XLA Ops:
  0.0 0.0 copy-start.3
  0.0 0.9 %copy-done.3 = bf16[1024,128]{1,0:T(8,128)(2,1)S(1)} copy-done((bf16[1024,128]{1,0:T(8,128)(2,1)S(1)}, bf16[1024,128]{1,0:T(8,128)(2,1)}, u32[]{:S(2)}) %copy-start.3) | copy-done | bytes 262168
  1.0 0.0 copy-start.4
  1.0 0.0 copy-start.5
  1.0 0.0 copy-start.6
  1.0 25.2 %spectra.1.t_ref = f32[4096,128]{1,0:T(8,128)} custom-call(bf16[1024,8,1024]{2,1,0:T(8,128)(2,1)} %x_ref.1, bf16[1024,128]{1,0:T(8,128)(2,1)S(1)} %copy-done.3), custom_call_target="tpu_custom_call" | custom-call | tf_op jit(solution)/shard_map/spectra/pallas_call | solution.py:281
  26.1 0.0 copy-done.4
  26.1 0.0 copy-done.5
  26.1 0.0 copy-done.6
  26.2 0.0 copy-start.2
  26.2 12.5 %image.1.i_ref = f32[4,128,128]{2,1,0:T(8,128)S(1)} custom-call(f32[4096,128]{1,0:T(8,128)} %spectra.1.t_ref, s32[4096]{0:T(1024)S(1)} %copy-done.4, s32[1024]{0:T(1024)S(1)} %copy-done.5, s32[1,4,16]{2,1,0:T(4,128)S(1)} %copy-done.6, f32[2,1,4,256,512]{4,3,2,1,0:T(8,128)} %left.1, f32[2,1,4,512,256]{4,3,2,1,0:T(8,128)} %right.1), custom_call_target="tpu_custom_call" | custom-call | tf_op jit(solution)/shard_map/image/pallas_call | solution.py:303
  38.7 0.0 copy-start.1
  38.7 0.7 %copy-done.1 = f32[4,128,128]{2,1,0:T(8,128)} copy-done((f32[4,128,128]{2,1,0:T(8,128)}, f32[4,128,128]{2,1,0:T(8,128)S(1)}, u32[]{:S(2)}) %copy-start.1) | copy-done | bytes 262168
  39.4 10.4 %giveback.1.x_ref = f32[4,128,128]{2,1,0:T(8,128)} custom-call(f32[4,128,128]{2,1,0:T(8,128)} %copy-done.1), custom_call_target="tpu_custom_call" | custom-call | tf_op jit(solution)/shard_map/giveback/pallas_call | solution.py:330
  49.9 0.0 copy-done.2
  49.9 0.0 copy-start
  49.9 0.9 %copy-done = f32[4,128,128]{2,1,0:T(8,128)S(1)} copy-done((f32[4,128,128]{2,1,0:T(8,128)S(1)}, f32[4,128,128]{2,1,0:T(8,128)}, u32[]{:S(2)}) %copy-start) | copy-done | bytes 262168
  50.8 12.4 %waves.1 = bf16[1,256,32,1024]{3,2,1,0:T(8,128)(2,1)} custom-call(f32[4,128,128]{2,1,0:T(8,128)S(1)} %copy-done, bf16[256,1024]{1,0:T(8,128)(2,1)S(1)} %copy-done.2), custom_call_target="tpu_custom_call" | custom-call | tf_op jit(solution)/shard_map/waves/pallas_call | solution.py:352
Async XLA Ops:
  0.0 0.9 %copy-start.3 = (bf16[1024,128]{1,0:T(8,128)(2,1)S(1)}, bf16[1024,128]{1,0:T(8,128)(2,1)}, u32[]{:S(2)}) copy-start(bf16[1024,128]{1,0:T(8,128)(2,1)} %constant.4.clone.w_ref) | copy-start | bytes 786436
  1.0 25.2 %copy-start.4 = (s32[4096]{0:T(1024)S(1)}, s32[4096]{0:T(1024)}, u32[]{:S(2)}) copy-start(s32[4096]{0:T(1024)} %smap.1) | copy-start | bytes 49156
  1.0 25.2 %copy-start.5 = (s32[1024]{0:T(1024)S(1)}, s32[1024]{0:T(1024)}, u32[]{:S(2)}) copy-start(s32[1024]{0:T(1024)} %rmap.1) | copy-start | bytes 12292
  1.0 25.2 %copy-start.6 = (s32[1,4,16]{2,1,0:T(4,128)S(1)}, s32[1,4,16]{2,1,0:T(4,128)}, u32[]{:S(2)}) copy-start(s32[1,4,16]{2,1,0:T(4,128)} %ranks.1) | copy-start | bytes 772
  26.2 23.7 %copy-start.2 = (bf16[256,1024]{1,0:T(8,128)(2,1)S(1)}, bf16[256,1024]{1,0:T(8,128)(2,1)}, u32[]{:S(2)}) copy-start(bf16[256,1024]{1,0:T(8,128)(2,1)} %constant.5.clone.w_ref) | copy-start | bytes 1572868
  38.7 0.7 %copy-start.1 = (f32[4,128,128]{2,1,0:T(8,128)}, f32[4,128,128]{2,1,0:T(8,128)S(1)}, u32[]{:S(2)}) copy-start(f32[4,128,128]{2,1,0:T(8,128)S(1)} %image.1.i_ref) | copy-start | bytes 786436
  49.9 1.0 %copy-start = (f32[4,128,128]{2,1,0:T(8,128)S(1)}, f32[4,128,128]{2,1,0:T(8,128)}, u32[]{:S(2)}) copy-start(f32[4,128,128]{2,1,0:T(8,128)} %giveback.1.x_ref) | copy-start | bytes 786436
where the time goes:
time: 63.4 us; the launch traced here: 63.2 us
  Pallas kernels  60.5 us (95%)
  local copies, waits for them, and re-layouts  2.61 us (4%)
    pallas_call x1, Pallas kernels, per_device(): pl.pallas_call(functools.partial(spectra_kernel, nf, n_rows, chunks), out...  25.2 us
    pallas_call x1, Pallas kernels, per_device(): pl.pallas_call(image_kernel, out_shape=jax.ShapeDtypeStruct((nf, per // 2...  12.5 us
    pallas_call x1, Pallas kernels, per_device(): pl.pallas_call(functools.partial(waves_kernel, nf, all_members), grid=(pe...  12.4 us
    pallas_call x1, Pallas kernels, per_device(): pl.pallas_call(functools.partial(return_kernel, nf), out_shape=jax.ShapeD...  10.4 us
    unnamed x14, local copies, waits for them, and re-layouts  2.61 us

commit v1 on v0

--- a/solution.py
+++ b/solution.py
@@ -45,7 +45,6 @@
     loads = []
     for c in range(chunks):
         load = pltpu.make_async_copy(x_ref.at[pl.ds(c * width, width)], xbuf.at[c], in_sem.at[c])
-        load.start()
         loads.append(load)
 
     barrier = pltpu.get_barrier_semaphore()
@@ -70,13 +69,15 @@
             send_sem=s1_send.at[c, d], recv_sem=s1_recv.at[c, d],
             device_id={"freq": to}, device_id_type=MESH)
 
-    def row_copy(c, m):
+    def row_copy(c, m, d):
         bit, off = messages[m]
-        block = land.at[c, flipped(r, off)]
+        block = land.at[c, flipped(r, off), lax.rem(z - d + nf, nf)]
         return pltpu.make_async_remote_copy(
             src_ref=block, dst_ref=block,
-            send_sem=h_send.at[c, m], recv_sem=h_recv.at[c, m],
+            send_sem=h_send.at[c, m, d], recv_sem=h_recv.at[c, m, d],
             device_id={"rows": flipped(r, bit)}, device_id_type=MESH)
+
+    first_hop = [m for m, (bit, off) in enumerate(messages) if off == 0]
 
     def compute(c):
         piece = 128
@@ -97,6 +98,8 @@
         land[c, r, z] = spec[c, z]
         for d in range(1, nf):
             band_copy(c, d).start()
+        for m in first_hop:
+            row_copy(c, m, 0).start()
 
     def turn(c):
         for zz in range(nf):
@@ -107,58 +110,62 @@
             full = jnp.concatenate(parts + again, axis=0)
             t_ref[zz * sources + c * width:zz * sources + (c + 1) * width, :] = full.T
 
-    stages = []
-    for m, (bit, off) in enumerate(messages):
-        stage = 0 if off == 0 else bits.__len__() - (off & -off).bit_length() + 1
-        stages.append(stage)
     depth = len(bits)
-    for step in range(chunks + depth + 1):
+    order = list(reversed(bits))
+    forward = [[m for m, (bit, off) in enumerate(messages) if off and (off & -off) == order[k]] for k in range(depth)]
+
+    def stage(k, c):
+        if k == 0:
+            for d in range(1, nf):
+                band_copy(c, d).wait_recv()
+                for m in first_hop:
+                    row_copy(c, m, d).start()
+            return
+        for d in range(nf):
+            for m, (bit, off) in enumerate(messages):
+                if bit == order[k - 1]:
+                    row_copy(c, m, d).wait_recv()
+            for m in forward[k - 1]:
+                row_copy(c, m, d).start()
+
+    ahead = min(2, chunks)
+    for c in range(ahead):
+        loads[c].start()
+    for step in range(chunks + depth + 3):
         if step < chunks:
             loads[step].wait()
             compute(step)
-        for stage in range(depth + 1):
-            c = step - 1 - stage
-            if not 0 <= c < chunks:
-                continue
-            if stage == 0:
-                for d in range(1, nf):
-                    band_copy(c, d).wait_recv()
-            else:
-                done_bit = bits[depth - stage]
-                for m, (bit, off) in enumerate(messages):
-                    if bit == done_bit:
-                        row_copy(c, m).wait_recv()
+            if step + ahead < chunks:
+                loads[step + ahead].start()
+        for k in range(depth + 1):
+            c = step - 2 - (k + 1 if k else 0)
+            if 0 <= c < chunks:
+                stage(k, c)
+                if k == depth:
+                    turn(c)
+    for c in range(chunks):
+        for d in range(nf):
+            if d:
+                band_copy(c, d).wait_send()
             for m in range(len(messages)):
-                if stages[m] == stage:
-                    row_copy(c, m).start()
-            if stage == depth:
-                turn(c)
-    for c in range(chunks):
-        for d in range(1, nf):
-            band_copy(c, d).wait_send()
-        for m in range(len(messages)):
-            row_copy(c, m).wait_send()
-
-
-def image_kernel(t_ref, smap, rmap, ranks, left, right, o_ref, cols, lbuf, rbuf, proj, img, even, odd, l_sem, r_sem):
+                row_copy(c, m, d).wait_send()
+
+
+def project_kernel(t_ref, smap, ranks, right, o_ref, cols, rbuf, proj, r_sem):
     slab = cols.shape[0]
     tile_rows, blocks = ranks.shape[1], ranks.shape[2]
     capacity, tile = right.shape[3], right.shape[4]
-    receivers = img.shape[0]
     loads_r = [[pltpu.make_async_copy(right.at[c, 0, i], rbuf.at[c, i, pl.ds(0, capacity)], r_sem.at[c, i])
                 for i in range(tile_rows)] for c in range(2)]
-    loads_l = [[pltpu.make_async_copy(left.at[c, 0, i], lbuf.at[c, i], l_sem.at[c, i])
-                for i in range(tile_rows)] for c in range(2)]
-    for loads in (loads_r, loads_l):
-        for i in range(tile_rows):
-            for c in range(2):
-                loads[c][i].start()
+    for i in range(tile_rows):
+        for c in range(2):
+            loads_r[c][i].start()
     proj[...] = jnp.zeros_like(proj)
 
-    @pl.loop(0, slab // 16)
+    @pl.loop(0, slab // 32)
     def _(g):
-        for u in range(16):
-            q = g * 16 + u
+        for u in range(32):
+            q = g * 32 + u
             cols[pl.ds(q, 1), :] = t_ref[pl.ds(smap[q], 1), :]
 
     for i in range(tile_rows):
@@ -181,7 +188,24 @@
     for i in range(tile_rows):
         proj[i, pl.ds(pl.multiple_of(starts[i], 8), RMAX), :] = jnp.zeros((RMAX, 128), jnp.float32)
     for i in range(tile_rows):
-        p = proj[i, :capacity, :]
+        o_ref[i] = proj[i, :capacity, :]
+
+
+def image_kernel(nf, p_ref, rmap, left, o_ref, lbuf, img, even, odd, out, l_sem, own_sem, send_sem, recv_sem):
+    z = lax.axis_index("freq")
+    tile_rows, tile = lbuf.shape[1], lbuf.shape[2]
+    receivers = img.shape[0]
+    pairs = out.shape[1]
+    loads_l = [[pltpu.make_async_copy(left.at[c, 0, i], lbuf.at[c, i], l_sem.at[c, i])
+                for i in range(tile_rows)] for c in range(2)]
+    for i in range(tile_rows):
+        for c in range(2):
+            loads_l[c][i].start()
+    barrier = pltpu.get_barrier_semaphore()
+    for d in range(1, nf):
+        pl.semaphore_signal(barrier, inc=1, device_id={"freq": lax.rem(z + d, nf)}, device_id_type=MESH)
+    for i in range(tile_rows):
+        p = p_ref[i]
         high = p.astype(jnp.bfloat16)
         low = (p - high.astype(jnp.float32)).astype(jnp.bfloat16)
         wide = jnp.concatenate([high, low], axis=1)
@@ -191,36 +215,31 @@
             prod = jnp.dot(lbuf[c, i].astype(jnp.bfloat16), wide, preferred_element_type=jnp.float32)
             sums.append(prod[:, :128] + prod[:, 128:])
         img[i * tile:(i + 1) * tile, :] = sums[0] + pltpu.roll(sums[1], 64, 1)
-
-    @pl.loop(0, receivers // 16)
-    def _(g):
-        for u in range(8):
-            n = g * 16 + 2 * u
-            even[pl.ds(g * 8 + u, 1), :] = img[pl.ds(lax.rem(rmap[n], receivers), 1), :]
-            odd[pl.ds(g * 8 + u, 1), :] = img[pl.ds(lax.rem(rmap[n + 1], receivers), 1), :]
-
-    lane2 = lax.broadcasted_iota(jnp.int32, even.shape, 1)
-    o_ref[...] = jnp.where(lane2 < 64, even[...], pltpu.roll(odd[...], 64, 1)).reshape(o_ref.shape)
-
-
-def return_kernel(nf, i_ref, o_ref, own_sem, send_sem, recv_sem):
-    z = lax.axis_index("freq")
-    own = pltpu.make_async_copy(i_ref.at[z], o_ref.at[z], own_sem)
-    own.start()
-    barrier = pltpu.get_barrier_semaphore()
-    for d in range(1, nf):
-        pl.semaphore_signal(barrier, inc=1, device_id={"freq": lax.rem(z + d, nf)}, device_id_type=MESH)
     pl.semaphore_wait(barrier, nf - 1)
+
     copies = []
-    for d in range(1, nf):
+    lane2 = lax.broadcasted_iota(jnp.int32, (pairs, 128), 1)
+    for d in list(range(1, nf)) + [0]:
         to = lax.rem(z + d, nf)
-        copy = pltpu.make_async_remote_copy(
-            src_ref=i_ref.at[to], dst_ref=o_ref.at[z],
-            send_sem=send_sem.at[d], recv_sem=recv_sem.at[d],
-            device_id={"freq": to}, device_id_type=MESH)
+        first = to * 2 * pairs
+
+        @pl.loop(0, pairs // 8)
+        def _(g):
+            for u in range(8):
+                n = first + g * 16 + 2 * u
+                even[d, pl.ds(g * 8 + u, 1), :] = img[pl.ds(lax.rem(rmap[n], receivers), 1), :]
+                odd[d, pl.ds(g * 8 + u, 1), :] = img[pl.ds(lax.rem(rmap[n + 1], receivers), 1), :]
+
+        out[d] = jnp.where(lane2 < 64, even[d], pltpu.roll(odd[d], 64, 1))
+        if d:
+            copy = pltpu.make_async_remote_copy(
+                src_ref=out.at[d], dst_ref=o_ref.at[z],
+                send_sem=send_sem.at[d], recv_sem=recv_sem.at[d],
+                device_id={"freq": to}, device_id_type=MESH)
+        else:
+            copy = pltpu.make_async_copy(out.at[0], o_ref.at[z], own_sem)
         copy.start()
         copies.append(copy)
-    own.wait()
     for copy in copies:
         copy.wait()
 
@@ -250,16 +269,19 @@
                 rows[parity, g, :, tile * 128:tile * 128 + 128] = acc
     sub = lax.broadcasted_iota(jnp.int32, (8, wide), 0)
     keep = lax.rem(lax.broadcasted_iota(jnp.int32, (8, wide), 1), 8) == sub
-    for n in range(2 * pairs):
-        parts = []
-        for g in range(groups):
-            row = rows[n % 2, g, pl.ds(n // 2, 1), :]
-            parts.append(jnp.where(keep, jnp.broadcast_to(row, (8, wide)), 0.0))
-        lhs[n * members:(n + 1) * members, :] = jnp.concatenate(parts, axis=0).astype(jnp.bfloat16)
-    step = 4
-    for n in range(0, 2 * pairs, step):
-        out = jnp.dot(lhs[n * members:(n + step) * members, :], w_ref[...], preferred_element_type=jnp.float32)
-        o_ref[0, n:n + step] = out.astype(jnp.bfloat16).reshape(step, members, out.shape[1])
+    half = pairs * members
+    cut = min(256, w_ref.shape[1])
+    for first in (0, pairs):
+        for n in range(first, first + pairs):
+            parts = []
+            for g in range(groups):
+                row = rows[n % 2, g, pl.ds(n // 2, 1), :]
+                parts.append(jnp.where(keep, jnp.broadcast_to(row, (8, wide)), 0.0))
+            lhs[n * members:(n + 1) * members, :] = jnp.concatenate(parts, axis=0).astype(jnp.bfloat16)
+        block = lhs[first * members:first * members + half, :]
+        for t in range(0, w_ref.shape[1], cut):
+            out = jnp.dot(block, w_ref[:, t:t + cut], preferred_element_type=jnp.float32)
+            o_ref[0, first:first + pairs, :, t:t + cut] = out.astype(jnp.bfloat16).reshape(pairs, members, cut)
 
 
 def per_device(traces, tile_ranks, source_map, receiver_map, left_factors, right_factors):
@@ -291,8 +313,8 @@
             pltpu.SemaphoreType.DMA((chunks,)),
             pltpu.SemaphoreType.DMA((chunks, nf)),
             pltpu.SemaphoreType.DMA((chunks, nf)),
-            pltpu.SemaphoreType.DMA((chunks, n_msg)),
-            pltpu.SemaphoreType.DMA((chunks, n_msg)),
+            pltpu.SemaphoreType.DMA((chunks, n_msg, nf)),
+            pltpu.SemaphoreType.DMA((chunks, n_msg, nf)),
         ],
         compiler_params=pltpu.CompilerParams(
             collective_id=0, has_side_effects=True, vmem_limit_bytes=VMEM_LIMIT),
@@ -300,46 +322,51 @@
     )(traces, jnp.asarray(w))
 
     per = receivers // nf
-    image = pl.pallas_call(
-        image_kernel,
-        out_shape=jax.ShapeDtypeStruct((nf, per // 2, 128), jnp.float32),
+    projected = pl.pallas_call(
+        project_kernel,
+        out_shape=jax.ShapeDtypeStruct((tile_rows, capacity, 128), jnp.float32),
         in_specs=[
             pl.BlockSpec(memory_space=pltpu.VMEM),
             pl.BlockSpec(memory_space=pltpu.SMEM),
             pl.BlockSpec(memory_space=pltpu.SMEM),
-            pl.BlockSpec(memory_space=pltpu.SMEM),
-            pl.BlockSpec(memory_space=pl.ANY),
             pl.BlockSpec(memory_space=pl.ANY),
         ],
         out_specs=pl.BlockSpec(memory_space=pltpu.VMEM),
         scratch_shapes=[
             pltpu.VMEM((slab, 128), jnp.float32),
-            pltpu.VMEM((2, tile_rows, tile, capacity), jnp.float32),
             pltpu.VMEM((2, tile_rows, capacity + RMAX, tile), jnp.float32),
             pltpu.VMEM((tile_rows, capacity + RMAX, 128), jnp.float32),
+            pltpu.SemaphoreType.DMA((2, tile_rows)),
+        ],
+        compiler_params=pltpu.CompilerParams(vmem_limit_bytes=VMEM_LIMIT),
+        name="project",
+    )(turned, source_map, tile_ranks, right_factors)
+
+    pairs = per // 2
+    returned = pl.pallas_call(
+        functools.partial(image_kernel, nf),
+        out_shape=jax.ShapeDtypeStruct((nf, pairs, 128), jnp.float32),
+        in_specs=[
+            pl.BlockSpec(memory_space=pltpu.VMEM),
+            pl.BlockSpec(memory_space=pltpu.SMEM),
+            pl.BlockSpec(memory_space=pl.ANY),
+        ],
+        out_specs=pl.BlockSpec(memory_space=pl.ANY),
+        scratch_shapes=[
+            pltpu.VMEM((2, tile_rows, tile, capacity), jnp.float32),
             pltpu.VMEM((receivers, 128), jnp.float32),
-            pltpu.VMEM((receivers // 2, 128), jnp.float32),
-            pltpu.VMEM((receivers // 2, 128), jnp.float32),
+            pltpu.VMEM((nf, pairs, 128), jnp.float32),
+            pltpu.VMEM((nf, pairs, 128), jnp.float32),
+            pltpu.VMEM((nf, pairs, 128), jnp.float32),
             pltpu.SemaphoreType.DMA((2, tile_rows)),
-            pltpu.SemaphoreType.DMA((2, tile_rows)),
-        ],
-        compiler_params=pltpu.CompilerParams(vmem_limit_bytes=VMEM_LIMIT),
-        name="image",
-    )(turned, source_map, receiver_map, tile_ranks, left_factors, right_factors)
-
-    returned = pl.pallas_call(
-        functools.partial(return_kernel, nf),
-        out_shape=jax.ShapeDtypeStruct(image.shape, jnp.float32),
-        in_specs=[pl.BlockSpec(memory_space=pltpu.VMEM)],
-        out_specs=pl.BlockSpec(memory_space=pltpu.VMEM),
-        scratch_shapes=[
             pltpu.SemaphoreType.DMA(()),
             pltpu.SemaphoreType.DMA((nf,)),
             pltpu.SemaphoreType.DMA((nf,)),
         ],
-        compiler_params=pltpu.CompilerParams(collective_id=1, has_side_effects=True),
-        name="giveback",
-    )(image)
+        compiler_params=pltpu.CompilerParams(
+            collective_id=1, has_side_effects=True, vmem_limit_bytes=VMEM_LIMIT),
+        name="image",
+    )(projected, receiver_map, left_factors)
 
     inverse = (basis / np.float32(math.sqrt(nf))).astype(np.float32)
     high = inverse.astype(jnp.bfloat16)
@@ -348,7 +375,7 @@
     wb = np.zeros((wide, samples), jnp.bfloat16)
     for part, table in enumerate((high, low, high)):
         wb[part * nf * 16:(part + 1) * nf * 16] = np.repeat(table.reshape(2 * nf, samples), 8, axis=0)
-    nb = 16
+    nb = min(64, per)
     return pl.pallas_call(
         functools.partial(waves_kernel, nf, all_members),
         grid=(per // nb,),

time: 63.4 us -> 52.9 us (0.83)
  Pallas kernels: 60.5 us -> 51.6 us
  local copies, waits for them, and re-layouts: 2.61 us -> 0.97 us
    pallas_call x2, Pallas kernels: 23 us -> 18.7 us  [the longest x1 12.3 us: per_device(): pl.pallas_call(functools.partial(image_kernel, nf), out_shape=jax.ShapeDt...]
    pallas_call x1, Pallas kernels: 12.4 us -> 8.11 us  [per_device(): pl.pallas_call(functools.partial(waves_kernel, nf, all_members), grid=(pe...]
    unnamed x14 -> x10, local copies, waits for them, and re-layouts: 2.61 us -> 0.97 us
where the time goes in v1:
time: 52.9 us; the launch traced here: 52.7 us
  Pallas kernels  51.6 us (98%)
  local copies, waits for them, and re-layouts  0.97 us (2%)
    pallas_call x1, Pallas kernels, per_device(): pl.pallas_call(functools.partial(spectra_kernel, nf, n_rows, chunks), out...  24.8 us
    pallas_call x1, Pallas kernels, per_device(): pl.pallas_call(functools.partial(image_kernel, nf), out_shape=jax.ShapeDt...  12.3 us
    pallas_call x1, Pallas kernels, per_device(): pl.pallas_call(functools.partial(waves_kernel, nf, all_members), grid=(pe...  8.11 us
    pallas_call x1, Pallas kernels, per_device(): pl.pallas_call(project_kernel, out_shape=jax.ShapeDtypeStruct((tile_rows,...  6.4 us

profile of v1, /device:TPU:0, one launch (start us, length us, event | category | flops | bytes accessed | tf_op | source)
XLA Modules:
  0.0 52.7 jit_solution(17105163937579418473)
XLA Ops:
  0.0 0.0 copy-start.1
  0.0 0.9 %copy-done.1 = bf16[1024,128]{1,0:T(8,128)(2,1)S(1)} copy-done((bf16[1024,128]{1,0:T(8,128)(2,1)S(1)}, bf16[1024,128]{1,0:T(8,128)(2,1)}, u32[]{:S(2)}) %copy-start.1) | copy-done | bytes 262168
  1.0 0.0 copy-start.2
  1.0 0.0 copy-start.4
  1.0 24.8 %spectra.1.t_ref = f32[4096,128]{1,0:T(8,128)} custom-call(bf16[1024,8,1024]{2,1,0:T(8,128)(2,1)} %x_ref.1, bf16[1024,128]{1,0:T(8,128)(2,1)S(1)} %copy-done.1), custom_call_target="tpu_custom_call" | custom-call | tf_op jit(solution)/shard_map/spectra/pallas_call | solution.py:303
  25.8 0.0 copy-done.2
  25.8 0.0 copy-done.4
  25.8 0.0 copy-start.3
  25.8 6.4 %project.1.p_ref = f32[4,512,128]{2,1,0:T(8,128)S(1)} custom-call(f32[4096,128]{1,0:T(8,128)} %spectra.1.t_ref, s32[4096]{0:T(1024)S(1)} %copy-done.2, s32[1,4,16]{2,1,0:T(4,128)S(1)} %copy-done.4, f32[2,1,4,512,256]{4,3,2,1,0:T(8,128)} %right.1), custom_call_target="tpu_custom_call" | custom-call | tf_op jit(solution)/shard_map/project/pallas_call | solution.py:325
  32.2 0.0 copy-done.3
  32.3 0.0 copy-start
  32.3 12.3 %image.1.x_ref = f32[4,128,128]{2,1,0:T(8,128)S(1)} custom-call(f32[4,512,128]{2,1,0:T(8,128)S(1)} %project.1.p_ref, s32[1024]{0:T(1024)S(1)} %copy-done.3, f32[2,1,4,256,512]{4,3,2,1,0:T(8,128)} %left.1), custom_call_target="tpu_custom_call" | custom-call | tf_op jit(solution)/shard_map/image/pallas_call | solution.py:346
  44.6 0.0 copy-done
  44.6 8.1 %waves.1 = bf16[1,256,32,1024]{3,2,1,0:T(8,128)(2,1)} custom-call(f32[4,128,128]{2,1,0:T(8,128)S(1)} %image.1.x_ref, bf16[256,1024]{1,0:T(8,128)(2,1)S(1)} %copy-done), custom_call_target="tpu_custom_call" | custom-call | tf_op jit(solution)/shard_map/waves/pallas_call | solution.py:379
Async XLA Ops:
  0.0 0.9 %copy-start.1 = (bf16[1024,128]{1,0:T(8,128)(2,1)S(1)}, bf16[1024,128]{1,0:T(8,128)(2,1)}, u32[]{:S(2)}) copy-start(bf16[1024,128]{1,0:T(8,128)(2,1)} %constant.4.clone.w_ref) | copy-start | bytes 786436
  1.0 24.9 %copy-start.2 = (s32[4096]{0:T(1024)S(1)}, s32[4096]{0:T(1024)}, u32[]{:S(2)}) copy-start(s32[4096]{0:T(1024)} %smap.1) | copy-start | bytes 49156
  1.0 24.9 %copy-start.4 = (s32[1,4,16]{2,1,0:T(4,128)S(1)}, s32[1,4,16]{2,1,0:T(4,128)}, u32[]{:S(2)}) copy-start(s32[1,4,16]{2,1,0:T(4,128)} %ranks.1) | copy-start | bytes 772
  25.8 6.4 %copy-start.3 = (s32[1024]{0:T(1024)S(1)}, s32[1024]{0:T(1024)}, u32[]{:S(2)}) copy-start(s32[1024]{0:T(1024)} %rmap.1) | copy-start | bytes 12292
  32.3 12.3 %copy-start = (bf16[256,1024]{1,0:T(8,128)(2,1)S(1)}, bf16[256,1024]{1,0:T(8,128)(2,1)}, u32[]{:S(2)}) copy-start(bf16[256,1024]{1,0:T(8,128)(2,1)} %constant.5.clone.w_ref) | copy-start | bytes 1572868

commit v2 on v1

--- a/solution.py
+++ b/solution.py
@@ -11,6 +11,7 @@
 
 RMAX = 32
 MESH = pl.DeviceIdType.MESH
+AHEAD = 2
 VMEM_LIMIT = 52 * 1024 * 1024
 
 
@@ -32,8 +33,8 @@
     return messages
 
 
-def spectra_kernel(nf, n_rows, chunks, x_ref, w_ref, t_ref, xbuf, sv, spec, land,
-                   in_sem, s1_send, s1_recv, h_send, h_recv):
+def spectra_kernel(nf, n_rows, chunks, x_ref, w_in, t_ref, w_ref, xbuf, sv, spec, land,
+                   in_sem, w_sem, s1_send, s1_recv, h_send, h_recv):
     z, r = lax.axis_index("freq"), lax.axis_index("rows")
     width, members = xbuf.shape[1], xbuf.shape[2]
     samples = xbuf.shape[3]
@@ -42,10 +43,15 @@
     messages = row_messages(n_rows)
     pair = 2 * members
 
+    w_load = pltpu.make_async_copy(w_in, w_ref, w_sem)
+    w_load.start()
     loads = []
     for c in range(chunks):
         load = pltpu.make_async_copy(x_ref.at[pl.ds(c * width, width)], xbuf.at[c], in_sem.at[c])
         loads.append(load)
+    ahead = min(AHEAD, chunks)
+    for c in range(ahead):
+        loads[c].start()
 
     barrier = pltpu.get_barrier_semaphore()
     bits = [1 << b for b in range(n_rows.bit_length() - 1)]
@@ -128,9 +134,7 @@
             for m in forward[k - 1]:
                 row_copy(c, m, d).start()
 
-    ahead = min(2, chunks)
-    for c in range(ahead):
-        loads[c].start()
+    w_load.wait()
     for step in range(chunks + depth + 3):
         if step < chunks:
             loads[step].wait()
@@ -291,7 +295,7 @@
     receivers = receiver_map.shape[0]
     all_members = members * n_rows
     tile_rows, capacity, tile = right_factors.shape[2:]
-    chunks = max(1, sources // 256)
+    chunks = max(1, sources // 512)
     width = sources // chunks
     basis = tables(samples, nf)
 
@@ -303,14 +307,16 @@
     turned = pl.pallas_call(
         functools.partial(spectra_kernel, nf, n_rows, chunks),
         out_shape=jax.ShapeDtypeStruct((slab, 128), jnp.float32),
-        in_specs=[pl.BlockSpec(memory_space=pl.ANY), pl.BlockSpec(memory_space=pltpu.VMEM)],
+        in_specs=[pl.BlockSpec(memory_space=pl.ANY)] * 2,
         out_specs=pl.BlockSpec(memory_space=pltpu.VMEM),
         scratch_shapes=[
+            pltpu.VMEM((samples, lanes), jnp.bfloat16),
             pltpu.VMEM((chunks, width, members, samples), jnp.bfloat16),
             pltpu.VMEM((lanes // 128, 128 * members, 128), jnp.float32),
             pltpu.VMEM((chunks, nf, 2 * members, width), jnp.float32),
             pltpu.VMEM((chunks, n_rows, nf, 2 * members, width), jnp.float32),
             pltpu.SemaphoreType.DMA((chunks,)),
+            pltpu.SemaphoreType.DMA(()),
             pltpu.SemaphoreType.DMA((chunks, nf)),
             pltpu.SemaphoreType.DMA((chunks, nf)),
             pltpu.SemaphoreType.DMA((chunks, n_msg, nf)),

time: 52.9 us -> 50.5 us (0.955)
  Pallas kernels: 51.6 us -> 49.3 us
    pallas_call x1, Pallas kernels: 24.8 us -> 22.6 us  [per_device(): pl.pallas_call(functools.partial(spectra_kernel, nf, n_rows, chunks), out...]
where the time goes in v2:
time: 50.5 us; the launch traced here: 50.4 us
  Pallas kernels  49.3 us (98%)
  local copies, waits for them, and re-layouts  0.97 us (2%)
    pallas_call x1, Pallas kernels, per_device(): pl.pallas_call(functools.partial(spectra_kernel, nf, n_rows, chunks), out...  22.6 us
    pallas_call x1, Pallas kernels, per_device(): pl.pallas_call(functools.partial(image_kernel, nf), out_shape=jax.ShapeDt...  12.2 us
    pallas_call x1, Pallas kernels, per_device(): pl.pallas_call(functools.partial(waves_kernel, nf, all_members), grid=(pe...  8.11 us
    pallas_call x1, Pallas kernels, per_device(): pl.pallas_call(project_kernel, out_shape=jax.ShapeDtypeStruct((tile_rows,...  6.4 us

profile of v2, /device:TPU:0, one launch (start us, length us, event | category | flops | bytes accessed | tf_op | source)
XLA Modules:
  0.0 50.4 jit_solution(16481777239419931751)
XLA Ops:
  0.0 0.0 copy-start.1
  0.0 0.9 %copy-done.1 = bf16[1024,128]{1,0:T(8,128)(2,1)S(1)} copy-done((bf16[1024,128]{1,0:T(8,128)(2,1)S(1)}, bf16[1024,128]{1,0:T(8,128)(2,1)}, u32[]{:S(2)}) %copy-start.1) | copy-done | bytes 262168
  1.0 0.0 copy-start.2
  1.0 0.0 copy-start.4
  1.0 22.6 %spectra.1.t_ref = f32[4096,128]{1,0:T(8,128)} custom-call(bf16[1024,8,1024]{2,1,0:T(8,128)(2,1)} %x_ref.1, bf16[1024,128]{1,0:T(8,128)(2,1)S(1)} %copy-done.1), custom_call_target="tpu_custom_call" | custom-call | tf_op jit(solution)/shard_map/spectra/pallas_call | solution.py:307
  23.5 0.0 copy-done.2
  23.6 0.0 copy-done.4
  23.6 0.0 copy-start.3
  23.6 6.4 %project.1.p_ref = f32[4,512,128]{2,1,0:T(8,128)S(1)} custom-call(f32[4096,128]{1,0:T(8,128)} %spectra.1.t_ref, s32[4096]{0:T(1024)S(1)} %copy-done.2, s32[1,4,16]{2,1,0:T(4,128)S(1)} %copy-done.4, f32[2,1,4,512,256]{4,3,2,1,0:T(8,128)} %right.1), custom_call_target="tpu_custom_call" | custom-call | tf_op jit(solution)/shard_map/project/pallas_call | solution.py:331
  30.0 0.0 copy-done.3
  30.0 0.0 copy-start
  30.0 12.2 %image.1.x_ref = f32[4,128,128]{2,1,0:T(8,128)S(1)} custom-call(f32[4,512,128]{2,1,0:T(8,128)S(1)} %project.1.p_ref, s32[1024]{0:T(1024)S(1)} %copy-done.3, f32[2,1,4,256,512]{4,3,2,1,0:T(8,128)} %left.1), custom_call_target="tpu_custom_call" | custom-call | tf_op jit(solution)/shard_map/image/pallas_call | solution.py:352
  42.3 0.0 copy-done
  42.3 8.1 %waves.1 = bf16[1,256,32,1024]{3,2,1,0:T(8,128)(2,1)} custom-call(f32[4,128,128]{2,1,0:T(8,128)S(1)} %image.1.x_ref, bf16[256,1024]{1,0:T(8,128)(2,1)S(1)} %copy-done), custom_call_target="tpu_custom_call" | custom-call | tf_op jit(solution)/shard_map/waves/pallas_call | solution.py:385
Async XLA Ops:
  0.0 0.9 %copy-start.1 = (bf16[1024,128]{1,0:T(8,128)(2,1)S(1)}, bf16[1024,128]{1,0:T(8,128)(2,1)}, u32[]{:S(2)}) copy-start(bf16[1024,128]{1,0:T(8,128)(2,1)} %constant.4.clone.w_in) | copy-start | bytes 786436
  1.0 22.6 %copy-start.2 = (s32[4096]{0:T(1024)S(1)}, s32[4096]{0:T(1024)}, u32[]{:S(2)}) copy-start(s32[4096]{0:T(1024)} %smap.1) | copy-start | bytes 49156
  1.0 22.6 %copy-start.4 = (s32[1,4,16]{2,1,0:T(4,128)S(1)}, s32[1,4,16]{2,1,0:T(4,128)}, u32[]{:S(2)}) copy-start(s32[1,4,16]{2,1,0:T(4,128)} %ranks.1) | copy-start | bytes 772
  23.6 6.4 %copy-start.3 = (s32[1024]{0:T(1024)S(1)}, s32[1024]{0:T(1024)}, u32[]{:S(2)}) copy-start(s32[1024]{0:T(1024)} %rmap.1) | copy-start | bytes 12292
  30.0 12.3 %copy-start = (bf16[256,1024]{1,0:T(8,128)(2,1)S(1)}, bf16[256,1024]{1,0:T(8,128)(2,1)}, u32[]{:S(2)}) copy-start(bf16[256,1024]{1,0:T(8,128)(2,1)} %constant.5.clone.w_ref) | copy-start | bytes 1572868
